TPU v7x, 32 devices: a whole 2x2x4 slice. The times are simulated.
32 devices in a mesh: sample: 2 (over y), wire: 4 (over z), xsec: 2 (over x), cols: 2 (over core).
Axes of the slice: x: 2, y: 2, z: 4, core: 2. Of those that a mesh axis runs over, the one named last changes fastest.
Arguments:
- blocks: bfloat16 [32, 2, 64, 1728], P(('sample', 'wire'), 'xsec'), parts along dimension 0, may hold values from -0.109375 to 0.109375
- pattern: int32 [32, 2, 27], P(('sample', 'wire'), 'xsec'), parts along dimension 0, may hold values 0 or 1
- current: bfloat16 [32, 2, 64, 2, 512], P(('sample', 'wire'), 'xsec', None, None, 'cols'), parts along dimension 0, may hold values from -6 to 6
- previous: bfloat16 [32, 2, 64, 2, 512], P(('sample', 'wire'), 'xsec', None, None, 'cols'), parts along dimension 0, may hold values from -6 to 6
- accum: float32 [32, 2, 64, 2, 512], P(('sample', 'wire'), 'xsec', None, None, 'cols'), parts along dimension 0, may hold values from -6 to 6
- coefs: float32 [4], replicated, may hold values from 0.3 to 1
- sketch: bfloat16 [32, 2, 64, 512], P(('sample', 'wire'), 'xsec'), parts along dimension 0, may hold values from -6 to 6
- signs: int32 [32, 2, 64, 512], P(('sample', 'wire'), 'xsec', None, 'cols'), parts along dimension 0, may hold values from 0 to 1
Outputs:
- newest: bfloat16 [32, 2, 64, 2, 512], P(('sample', 'wire'), 'xsec', None, None, 'cols'), parts along dimension 0
- before: bfloat16 [32, 2, 64, 2, 512], P(('sample', 'wire'), 'xsec', None, None, 'cols'), parts along dimension 0
- summed: float32 [32, 2, 64, 2, 512], P(('sample', 'wire'), 'xsec', None, None, 'cols'), parts along dimension 0
- gram: float32 [1024, 512], P(('sample', 'wire', 'xsec'), 'cols'), parts along dimension 0
- quadratic: float32 [1024], P(('sample', 'cols')), parts along dimension 0
There are 2 independent parts, one for each index of `sample`. A program takes and returns all parts, laid end to end along the dimension named above; an argument that names none is the same for every part. Nothing has to cross between parts.
All inputs are finite; a program needn't handle non-finite values. No bound on the sum of `pattern` on one device may be relied on, other than what follows from the above.
Results may differ from a plain program's by a relative error of at most 0.0065.
Values may be sent and summed in bfloat16 or wider, within the bound.
A program may use at most 64 MiB of HBM per device.

v0:
```python
import jax
import jax.numpy as jnp
from jax import lax
from jax.sharding import PartitionSpec as P

REACH = 4
STEPS = 4


def padded(x, sides, width, wrap):
    for axis, dim in sides:
        size, length = (lax.axis_size(axis), x.shape[dim])
        up = [(i, (i + 1) % size) for i in range(size if wrap else size - 1)]
        down = [(j, i) for i, j in up]
        last = lax.slice_in_dim(x, length - width, length, axis=dim)
        initial = lax.slice_in_dim(x, 0, width, axis=dim)
        before = lax.ppermute(last, axis, up)
        after = lax.ppermute(initial, axis, down)
        x = jnp.concatenate([before, x, after], axis=dim)
    return x


def apply_operator(field, masked):
    cells, tiles, orbs, halves, local_cols = field.shape
    reach = REACH
    lengthened = padded(field, (("wire", 0),), reach, True)
    extended = padded(lengthened, (("xsec", 1),), 1, False)
    flat_ext = extended.reshape(cells + 2 * reach, tiles + 2, orbs, halves * local_cols)
    total = jnp.zeros((cells, tiles, orbs, halves * local_cols), jnp.float32)
    for shift_d in range(2 * reach + 1):
        for shift_e in range(3):
            column = shift_d * 3 + shift_e
            piece = flat_ext[shift_d : shift_d + cells, shift_e : shift_e + tiles]
            part = masked[:, :, :, column * orbs : (column + 1) * orbs]
            total = total + jnp.einsum(
                "ctik,ctkn->ctin", part, piece, preferred_element_type=jnp.float32
            )
    return total.reshape(cells, tiles, orbs, halves, local_cols)


def body(blocks, pattern, current, previous, accum, coefs, sketch, signs):
    cells, tiles, orbs, wide = blocks.shape
    count = wide // orbs
    masked = (
        blocks.reshape(cells, tiles, orbs, count, orbs)
        * pattern.astype(jnp.bfloat16)[:, :, None, :, None]
    ).reshape(cells, tiles, orbs, wide)
    for step in range(STEPS):
        image = apply_operator(current, masked)
        nxt = (2.0 * image - previous.astype(jnp.float32)).astype(jnp.bfloat16)
        accum = accum + coefs[step] * nxt.astype(jnp.float32)
        previous = current
        current = nxt
    cells, tiles, orbs, halves, local_cols = accum.shape
    all_rows = cells * lax.axis_size("wire") * tiles * lax.axis_size("xsec") * orbs
    scale = jnp.float32(1.0) / jnp.sqrt(jnp.float32(all_rows))
    sketched = accum[:, :, :, 0, :].astype(jnp.bfloat16).reshape(cells * tiles * orbs, local_cols)
    omega = sketch.reshape(cells * tiles * orbs, sketch.shape[3])
    partial_gram = lax.dot_general(
        omega, sketched, (((0,), (0,)), ((), ())), preferred_element_type=jnp.float32
    )
    gram = lax.psum_scatter(partial_gram, ("wire", "xsec"), scatter_dimension=0, tiled=True) * scale
    plus_minus = (2 * signs - 1).astype(jnp.float32)
    local_quad = jnp.sum(plus_minus * accum[:, :, :, 1, :], axis=(0, 1, 2))
    quadratic = lax.psum(local_quad, ("wire", "xsec")) * scale
    return (current, previous, accum, gram, quadratic)


def solution(mesh):
    return jax.shard_map(
        body,
        mesh=mesh,
        in_specs=(
            P(("sample", "wire"), "xsec", None, None),
            P(("sample", "wire"), "xsec", None),
            P(("sample", "wire"), "xsec", None, None, "cols"),
            P(("sample", "wire"), "xsec", None, None, "cols"),
            P(("sample", "wire"), "xsec", None, None, "cols"),
            P(),
            P(("sample", "wire"), "xsec", None, None),
            P(("sample", "wire"), "xsec", None, "cols"),
        ),
        out_specs=(
            P(("sample", "wire"), "xsec", None, None, "cols"),
            P(("sample", "wire"), "xsec", None, None, "cols"),
            P(("sample", "wire"), "xsec", None, None, "cols"),
            P(("sample", "wire", "xsec"), "cols"),
            P(("sample", "cols")),
        ),
        check_vma=False,
    )
```

profile of v0, /device:TPU:0, one launch (start us, length us, event | category | flops | bytes accessed | tf_op | source)
XLA Modules:
  0.0 266.6 jit_solution(3019702308393329979)
XLA Ops:
  7.2 3.1 %collective-permute-start = (bf16[4,1,64,2,256]{4,3,2,1,0:T(2,128)(2,1)}, bf16[4,1,64,2,256]{4,3,2,1,0:T(2,128)(2,1)S(1)}, u32[]{:S(2)}, u32[]{:S(2)}) collective-permute-start(bf16[4,1,64,2,256]{4,3,2,1,0:T(2,128)(2,1)} %param.10), channel_id=1, source_target_pairs={{0,4},{4,8},{8,12},{12,0},{1,5},{5,9},{9,13},{13,1},{2,6},{6,10},{... | collective-permute-start | bytes 786440 | tf_op jit(solution)/shard_map/ppermute | solution.py:17
  10.3 2.1 collective-permute-start.1
  12.4 7.3 %collective-permute-done = bf16[4,1,64,2,256]{4,3,2,1,0:T(2,128)(2,1)S(1)} collective-permute-done((bf16[4,1,64,2,256]{4,3,2,1,0:T(2,128)(2,1)}, bf16[4,1,64,2,256]{4,3,2,1,0:T(2,128)(2,1)S(1)}, u32[]{:S(2)}, u32[]{:S(2)}) %collective-permute-start) | collective-permute-done | bytes 262176 | tf_op jit(solution)/shard_map/ppermute | solution.py:17
  19.9 1.2 constant_dynamic-update-slice_fusion.1
  21.1 2.8 %collective-permute-done.1 = bf16[4,1,64,2,256]{4,3,2,1,0:T(2,128)(2,1)S(1)} collective-permute-done((bf16[4,1,64,2,256]{4,3,2,1,0:T(2,128)(2,1)}, bf16[4,1,64,2,256]{4,3,2,1,0:T(2,128)(2,1)S(1)}, u32[]{:S(2)}, u32[]{:S(2)}) %collective-permute-start.1) | collective-permute-done | bytes 262176 | tf_op jit(solution)/shard_map/ppermute | solution.py:18
  24.1 3.4 %collective-permute-start.2 = (bf16[12,1,64,2,256]{4,3,2,1,0:T(2,128)(2,1)S(1)}, bf16[12,1,64,2,256]{4,3,2,1,0:T(2,128)(2,1)S(1)}, u32[]{:S(2)}, u32[]{:S(2)}) collective-permute-start(bf16[12,1,64,2,256]{4,3,2,1,0:T(2,128)(2,1)S(1)} %constant_dynamic-update-slice_fusion), channel_id=1, source_target_pairs={{0,2},{1,3},{4,6},{5,7},{8,10},{9,11},{12,14},{13,15},{16,18},{17,... | collective-permute-start | bytes 2359304 | tf_op jit(solution)/shard_map/ppermute | solution.py:17
  27.6 1.3 collective-permute-start.3
  28.9 0.7 convert_element_type.47
  29.7 1.2 bitcast_multiply_fusion
  31.0 12.9 %collective-permute-done.2 = bf16[12,1,64,2,256]{4,3,2,1,0:T(2,128)(2,1)S(1)} collective-permute-done((bf16[12,1,64,2,256]{4,3,2,1,0:T(2,128)(2,1)S(1)}, bf16[12,1,64,2,256]{4,3,2,1,0:T(2,128)(2,1)S(1)}, u32[]{:S(2)}, u32[]{:S(2)}) %collective-permute-start.2) | collective-permute-done | bytes 786464 | tf_op jit(solution)/shard_map/ppermute | solution.py:17
  43.8 4.2 %collective-permute-done.3 = bf16[12,1,64,2,256]{4,3,2,1,0:T(2,128)(2,1)S(1)} collective-permute-done((bf16[12,1,64,2,256]{4,3,2,1,0:T(2,128)(2,1)S(1)}, bf16[12,1,64,2,256]{4,3,2,1,0:T(2,128)(2,1)S(1)}, u32[]{:S(2)}, u32[]{:S(2)}) %collective-permute-start.3) | collective-permute-done | bytes 786464 | tf_op jit(solution)/shard_map/ppermute | solution.py:18
  48.0 4.6 %pad_maximum_fusion = bf16[12,3,64,2,256]{4,3,2,1,0:T(2,128)(2,1)} fusion(bf16[12,1,64,2,256]{4,3,2,1,0:T(2,128)(2,1)S(1)} %collective-permute-done.3, bf16[12,1,64,2,256]{4,3,2,1,0:T(2,128)(2,1)S(1)} %constant_dynamic-update-slice_fusion, bf16[12,1,64,2,256]{4,3,2,1,0:T(2,128)(2,1)S(1)} %collective-permute-done.2), kind=kLoop, calls=%fused_computation | loop fusion | flops 2359296 | bytes 4718592 | tf_op jit(solution)/shard_map/concatenate | solution.py:19
  52.6 5.3 %reshape.948 = bf16[12,3,64,512]{3,2,1,0:T(8,128)(2,1)S(1)} reshape(bf16[12,3,64,2,256]{4,3,2,1,0:T(2,128)(2,1)} %pad_maximum_fusion) | data formatting | bytes 4718592 | tf_op jit(solution)/shard_map/reshape | solution.py:28
  58.6 0.3 convolution_add_fusion.101
  59.6 0.3 convolution_add_fusion.97
  60.1 0.3 convolution_add_fusion.95
  64.2 1.0 fusion.3
  65.2 1.4 mul.124
  66.6 1.0 fusion.11
  67.6 1.8 collective-permute-start.4
  69.4 2.1 collective-permute-start.5
  71.5 7.2 %collective-permute-done.4 = bf16[4,1,64,2,256]{4,2,0,3,1:T(8,128)(2,1)S(1)} collective-permute-done((bf16[4,1,64,2,256]{4,2,0,3,1:T(8,128)(2,1)S(1)}, bf16[4,1,64,2,256]{4,2,0,3,1:T(8,128)(2,1)S(1)}, u32[]{:S(2)}, u32[]{:S(2)}) %collective-permute-start.4) | collective-permute-done | bytes 262176 | tf_op jit(solution)/shard_map/ppermute | solution.py:17
  78.7 2.8 %collective-permute-done.5 = bf16[4,1,64,2,256]{4,2,0,3,1:T(8,128)(2,1)S(1)} collective-permute-done((bf16[4,1,64,2,256]{4,2,0,3,1:T(8,128)(2,1)S(1)}, bf16[4,1,64,2,256]{4,2,0,3,1:T(8,128)(2,1)S(1)}, u32[]{:S(2)}, u32[]{:S(2)}) %collective-permute-start.5) | collective-permute-done | bytes 262176 | tf_op jit(solution)/shard_map/ppermute | solution.py:18
  81.6 1.5 collective-permute-start.6
  83.1 1.3 collective-permute-start.7
  84.4 15.7 %collective-permute-done.6 = bf16[12,1,64,2,256]{4,2,0,3,1:T(8,128)(2,1)S(1)} collective-permute-done((bf16[12,1,64,2,256]{4,2,0,3,1:T(8,128)(2,1)S(1)}, bf16[12,1,64,2,256]{4,2,0,3,1:T(8,128)(2,1)S(1)}, u32[]{:S(2)}, u32[]{:S(2)}) %collective-permute-start.6) | collective-permute-done | bytes 786464 | tf_op jit(solution)/shard_map/ppermute | solution.py:17
  100.1 4.2 %collective-permute-done.7 = bf16[12,1,64,2,256]{4,2,0,3,1:T(8,128)(2,1)S(1)} collective-permute-done((bf16[12,1,64,2,256]{4,2,0,3,1:T(8,128)(2,1)S(1)}, bf16[12,1,64,2,256]{4,2,0,3,1:T(8,128)(2,1)S(1)}, u32[]{:S(2)}, u32[]{:S(2)}) %collective-permute-start.7) | collective-permute-done | bytes 786464 | tf_op jit(solution)/shard_map/ppermute | solution.py:18
  104.3 0.3 maximum_bitcast_fusion
  105.0 0.3 convolution_add_fusion.77
  110.9 0.3 convolution_add_fusion.53
  111.4 0.3 mul.126
  111.8 0.6 collective-permute-start.8
  112.4 3.2 %collective-permute-start.9 = (bf16[4,1,64,2,256]{4,2,0,3,1:T(8,128)(2,1)S(1)}, bf16[4,1,64,2,256]{4,2,0,3,1:T(8,128)(2,1)S(1)}, u32[]{:S(2)}, u32[]{:S(2)}) collective-permute-start(bf16[4,1,64,2,256]{4,2,0,3,1:T(8,128)(2,1)S(1)} %fusion.10), channel_id=1, source_target_pairs={{4,0},{8,4},{12,8},{0,12},{5,1},{9,5},{13,9},{1,13},{6,2},{10,6},{... | collective-permute-start | bytes 786440 | tf_op jit(solution)/shard_map/ppermute | solution.py:18
  115.7 7.2 %collective-permute-done.8 = bf16[4,1,64,2,256]{4,2,0,3,1:T(8,128)(2,1)S(1)} collective-permute-done((bf16[4,1,64,2,256]{4,2,0,3,1:T(8,128)(2,1)S(1)}, bf16[4,1,64,2,256]{4,2,0,3,1:T(8,128)(2,1)S(1)}, u32[]{:S(2)}, u32[]{:S(2)}) %collective-permute-start.8) | collective-permute-done | bytes 262176 | tf_op jit(solution)/shard_map/ppermute | solution.py:17
  122.9 2.0 collective-permute-done.9
  125.0 1.5 collective-permute-start.10
  126.5 1.3 collective-permute-start.11
  127.8 14.2 %collective-permute-done.10 = bf16[12,1,64,2,256]{4,2,0,3,1:T(8,128)(2,1)S(1)} collective-permute-done((bf16[12,1,64,2,256]{4,2,0,3,1:T(8,128)(2,1)S(1)}, bf16[12,1,64,2,256]{4,2,0,3,1:T(8,128)(2,1)S(1)}, u32[]{:S(2)}, u32[]{:S(2)}) %collective-permute-start.10) | collective-permute-done | bytes 786464 | tf_op jit(solution)/shard_map/ppermute | solution.py:17
  142.0 4.2 %collective-permute-done.11 = bf16[12,1,64,2,256]{4,2,0,3,1:T(8,128)(2,1)S(1)} collective-permute-done((bf16[12,1,64,2,256]{4,2,0,3,1:T(8,128)(2,1)S(1)}, bf16[12,1,64,2,256]{4,2,0,3,1:T(8,128)(2,1)S(1)}, u32[]{:S(2)}, u32[]{:S(2)}) %collective-permute-start.11) | collective-permute-done | bytes 786464 | tf_op jit(solution)/shard_map/ppermute | solution.py:18
  146.1 0.3 maximum_bitcast_fusion.1
  153.2 0.3 mul.128
  153.6 0.6 collective-permute-start.12
  154.2 3.3 %collective-permute-start.13 = (bf16[4,1,64,2,256]{4,2,0,3,1:T(8,128)(2,1)S(1)}, bf16[4,1,64,2,256]{4,2,0,3,1:T(8,128)(2,1)S(1)}, u32[]{:S(2)}, u32[]{:S(2)}) collective-permute-start(bf16[4,1,64,2,256]{4,2,0,3,1:T(8,128)(2,1)S(1)} %fusion.4), channel_id=1, source_target_pairs={{4,0},{8,4},{12,8},{0,12},{5,1},{9,5},{13,9},{1,13},{6,2},{10,6},{... | collective-permute-start | bytes 786440 | tf_op jit(solution)/shard_map/ppermute | solution.py:18
  157.5 6.6 %collective-permute-done.12 = bf16[4,1,64,2,256]{4,2,0,3,1:T(8,128)(2,1)S(1)} collective-permute-done((bf16[4,1,64,2,256]{4,2,0,3,1:T(8,128)(2,1)S(1)}, bf16[4,1,64,2,256]{4,2,0,3,1:T(8,128)(2,1)S(1)}, u32[]{:S(2)}, u32[]{:S(2)}) %collective-permute-start.12) | collective-permute-done | bytes 262176 | tf_op jit(solution)/shard_map/ppermute | solution.py:17
  164.1 1.1 collective-permute-done.13
  165.3 1.5 collective-permute-start.14
  166.8 1.3 collective-permute-start.15
  168.1 0.6 fusion.24
  168.7 12.2 %collective-permute-done.14 = bf16[12,1,64,2,256]{4,2,0,3,1:T(8,128)(2,1)S(1)} collective-permute-done((bf16[12,1,64,2,256]{4,2,0,3,1:T(8,128)(2,1)S(1)}, bf16[12,1,64,2,256]{4,2,0,3,1:T(8,128)(2,1)S(1)}, u32[]{:S(2)}, u32[]{:S(2)}) %collective-permute-start.14) | collective-permute-done | bytes 786464 | tf_op jit(solution)/shard_map/ppermute | solution.py:17
  180.9 4.2 %collective-permute-done.15 = bf16[12,1,64,2,256]{4,2,0,3,1:T(8,128)(2,1)S(1)} collective-permute-done((bf16[12,1,64,2,256]{4,2,0,3,1:T(8,128)(2,1)S(1)}, bf16[12,1,64,2,256]{4,2,0,3,1:T(8,128)(2,1)S(1)}, u32[]{:S(2)}, u32[]{:S(2)}) %collective-permute-start.15) | collective-permute-done | bytes 786464 | tf_op jit(solution)/shard_map/ppermute | solution.py:18
  185.0 0.3 maximum_bitcast_fusion.2
  185.8 0.3 convolution_add_fusion.25
  191.6 0.3 convolution_add_fusion.1
  192.1 0.3 mul.130
  192.5 2.8 %fusion.8 = (f32[4,1,64,2,256]{4,2,0,3,1:T(8,128)S(1)}, bf16[4,1,64,2,256]{4,2,0,3,1:T(8,128)(2,1)S(1)}) fusion(bf16[4,1,64,2,256]{4,2,0,3,1:T(8,128)(2,1)S(1)} %fusion.11, bf16[4,1,64,2,256]{4,2,0,3,1:T(8,128)(2,1)S(1)} %fusion.10, f32[4,1,64,2,256]{4,3,2,1,0:T(2,128)S(1)} %copy-done.2, bf16[4,1,64,2,256]{4,2,0,3,1:T(8,128)(2,1)S(1)} %fusion.4, ...), kind=kLoop, calls=%fused_computation.125 | loop fusion | flops 1835008 | bytes 2621456 | tf_op jit(solution)/shard_map/add | solution.py:51
  195.6 1.0 copy.65
  196.6 1.0 copy.61
  197.6 1.2 copy.62
  198.8 1.0 copy.60
  199.8 17.8 %psum.7 = f32[256]{0:T(256)S(1)} all-reduce(f32[256]{0:T(256)S(1)} %fusion.13), channel_id=1, replica_groups=mesh['sample'=2,'wire'=4,'xsec'=2,'cols'=2] {'wire','xsec'}, use_global_device_ids=true, to_apply=%region_2.0 | all-reduce | flops 256 | bytes 2048 | tf_op jit(solution)/shard_map/psum | solution.py:65
  217.6 0.6 broadcast_multiply_fusion.1
  218.2 39.9 %reduce-scatter.4.cloned.1.call-done = f32[64,256]{1,0:T(8,128)} async-done(((f32[512,256]{1,0:T(8,128)}), f32[64,256]{1,0:T(8,128)}) %reduce-scatter.4.cloned.1.call-update) | async-done | bytes 65552
  258.0 0.9 copy.66
  259.0 0.7 copy.63
  (128 shorter events, 25.4 us)
Async XLA Ops:
  7.2 188.1 %copy-start = (bf16[4,1,64,512]{3,2,1,0:T(8,128)(2,1)S(1)}, bf16[4,1,64,512]{3,2,1,0:T(8,128)(2,1)}, u32[]{:S(2)}) copy-start(bf16[4,1,64,512]{3,2,1,0:T(8,128)(2,1)} %param.14) | copy-start | bytes 786436
  7.2 250.9 %reduce-scatter.4.cloned.1.call-start = ((), (), s32[]{:S(2)}) async-start(), calls=%async_computation.1 | async-start | bytes 589824
  7.2 12.5 %collective-permute-start = (bf16[4,1,64,2,256]{4,3,2,1,0:T(2,128)(2,1)}, bf16[4,1,64,2,256]{4,3,2,1,0:T(2,128)(2,1)S(1)}, u32[]{:S(2)}, u32[]{:S(2)}) collective-permute-start(bf16[4,1,64,2,256]{4,3,2,1,0:T(2,128)(2,1)} %param.10), channel_id=1, source_target_pairs={{0,4},{4,8},{8,12},{12,0},{1,5},{5,9},{9,13},{13,1},{2,6},{6,10},{... | collective-permute-start | bytes 786440 | tf_op jit(solution)/shard_map/ppermute | solution.py:17
  10.3 13.6 %collective-permute-start.1 = (bf16[4,1,64,2,256]{4,3,2,1,0:T(2,128)(2,1)}, bf16[4,1,64,2,256]{4,3,2,1,0:T(2,128)(2,1)S(1)}, u32[]{:S(2)}, u32[]{:S(2)}) collective-permute-start(bf16[4,1,64,2,256]{4,3,2,1,0:T(2,128)(2,1)} %param.10), channel_id=1, source_target_pairs={{4,0},{8,4},{12,8},{0,12},{5,1},{9,5},{13,9},{1,13},{6,2},{10,6},{... | collective-permute-start | bytes 786440 | tf_op jit(solution)/shard_map/ppermute | solution.py:18
  24.1 19.7 %collective-permute-start.2 = (bf16[12,1,64,2,256]{4,3,2,1,0:T(2,128)(2,1)S(1)}, bf16[12,1,64,2,256]{4,3,2,1,0:T(2,128)(2,1)S(1)}, u32[]{:S(2)}, u32[]{:S(2)}) collective-permute-start(bf16[12,1,64,2,256]{4,3,2,1,0:T(2,128)(2,1)S(1)} %constant_dynamic-update-slice_fusion), channel_id=1, source_target_pairs={{0,2},{1,3},{4,6},{5,7},{8,10},{9,11},{12,14},{13,15},{16,18},{17,... | collective-permute-start | bytes 2359304 | tf_op jit(solution)/shard_map/ppermute | solution.py:17
  27.6 20.5 %collective-permute-start.3 = (bf16[12,1,64,2,256]{4,3,2,1,0:T(2,128)(2,1)S(1)}, bf16[12,1,64,2,256]{4,3,2,1,0:T(2,128)(2,1)S(1)}, u32[]{:S(2)}, u32[]{:S(2)}) collective-permute-start(bf16[12,1,64,2,256]{4,3,2,1,0:T(2,128)(2,1)S(1)} %constant_dynamic-update-slice_fusion), channel_id=1, source_target_pairs={{2,0},{3,1},{6,4},{7,5},{10,8},{11,9},{14,12},{15,13},{18,16},{19,... | collective-permute-start | bytes 2359304 | tf_op jit(solution)/shard_map/ppermute | solution.py:18
  67.6 11.1 %collective-permute-start.4 = (bf16[4,1,64,2,256]{4,2,0,3,1:T(8,128)(2,1)S(1)}, bf16[4,1,64,2,256]{4,2,0,3,1:T(8,128)(2,1)S(1)}, u32[]{:S(2)}, u32[]{:S(2)}) collective-permute-start(bf16[4,1,64,2,256]{4,2,0,3,1:T(8,128)(2,1)S(1)} %fusion.11), channel_id=1, source_target_pairs={{0,4},{4,8},{8,12},{12,0},{1,5},{5,9},{9,13},{13,1},{2,6},{6,10},{... | collective-permute-start | bytes 786440 | tf_op jit(solution)/shard_map/ppermute | solution.py:17
  69.4 12.1 %collective-permute-start.5 = (bf16[4,1,64,2,256]{4,2,0,3,1:T(8,128)(2,1)S(1)}, bf16[4,1,64,2,256]{4,2,0,3,1:T(8,128)(2,1)S(1)}, u32[]{:S(2)}, u32[]{:S(2)}) collective-permute-start(bf16[4,1,64,2,256]{4,2,0,3,1:T(8,128)(2,1)S(1)} %fusion.11), channel_id=1, source_target_pairs={{4,0},{8,4},{12,8},{0,12},{5,1},{9,5},{13,9},{1,13},{6,2},{10,6},{... | collective-permute-start | bytes 786440 | tf_op jit(solution)/shard_map/ppermute | solution.py:18
  81.6 18.5 %collective-permute-start.6 = (bf16[12,1,64,2,256]{4,2,0,3,1:T(8,128)(2,1)S(1)}, bf16[12,1,64,2,256]{4,2,0,3,1:T(8,128)(2,1)S(1)}, u32[]{:S(2)}, u32[]{:S(2)}) collective-permute-start(bf16[12,1,64,2,256]{4,2,0,3,1:T(8,128)(2,1)S(1)} %pad_maximum_fusion.1), channel_id=1, source_target_pairs={{0,2},{1,3},{4,6},{5,7},{8,10},{9,11},{12,14},{13,15},{16,18},{17,... | collective-permute-start | bytes 2359304 | tf_op jit(solution)/shard_map/ppermute | solution.py:17
  83.1 21.1 %collective-permute-start.7 = (bf16[12,1,64,2,256]{4,2,0,3,1:T(8,128)(2,1)S(1)}, bf16[12,1,64,2,256]{4,2,0,3,1:T(8,128)(2,1)S(1)}, u32[]{:S(2)}, u32[]{:S(2)}) collective-permute-start(bf16[12,1,64,2,256]{4,2,0,3,1:T(8,128)(2,1)S(1)} %pad_maximum_fusion.1), channel_id=1, source_target_pairs={{2,0},{3,1},{6,4},{7,5},{10,8},{11,9},{14,12},{15,13},{18,16},{19,... | collective-permute-start | bytes 2359304 | tf_op jit(solution)/shard_map/ppermute | solution.py:18
  110.6 1.1 copy-start.1
  111.8 11.1 %collective-permute-start.8 = (bf16[4,1,64,2,256]{4,2,0,3,1:T(8,128)(2,1)S(1)}, bf16[4,1,64,2,256]{4,2,0,3,1:T(8,128)(2,1)S(1)}, u32[]{:S(2)}, u32[]{:S(2)}) collective-permute-start(bf16[4,1,64,2,256]{4,2,0,3,1:T(8,128)(2,1)S(1)} %fusion.10), channel_id=1, source_target_pairs={{0,4},{4,8},{8,12},{12,0},{1,5},{5,9},{9,13},{13,1},{2,6},{6,10},{... | collective-permute-start | bytes 786440 | tf_op jit(solution)/shard_map/ppermute | solution.py:17
  112.4 12.5 %collective-permute-start.9 = (bf16[4,1,64,2,256]{4,2,0,3,1:T(8,128)(2,1)S(1)}, bf16[4,1,64,2,256]{4,2,0,3,1:T(8,128)(2,1)S(1)}, u32[]{:S(2)}, u32[]{:S(2)}) collective-permute-start(bf16[4,1,64,2,256]{4,2,0,3,1:T(8,128)(2,1)S(1)} %fusion.10), channel_id=1, source_target_pairs={{4,0},{8,4},{12,8},{0,12},{5,1},{9,5},{13,9},{1,13},{6,2},{10,6},{... | collective-permute-start | bytes 786440 | tf_op jit(solution)/shard_map/ppermute | solution.py:18
  125.0 17.0 %collective-permute-start.10 = (bf16[12,1,64,2,256]{4,2,0,3,1:T(8,128)(2,1)S(1)}, bf16[12,1,64,2,256]{4,2,0,3,1:T(8,128)(2,1)S(1)}, u32[]{:S(2)}, u32[]{:S(2)}) collective-permute-start(bf16[12,1,64,2,256]{4,2,0,3,1:T(8,128)(2,1)S(1)} %pad_maximum_fusion.2), channel_id=1, source_target_pairs={{0,2},{1,3},{4,6},{5,7},{8,10},{9,11},{12,14},{13,15},{16,18},{17,... | collective-permute-start | bytes 2359304 | tf_op jit(solution)/shard_map/ppermute | solution.py:17
  126.5 19.6 %collective-permute-start.11 = (bf16[12,1,64,2,256]{4,2,0,3,1:T(8,128)(2,1)S(1)}, bf16[12,1,64,2,256]{4,2,0,3,1:T(8,128)(2,1)S(1)}, u32[]{:S(2)}, u32[]{:S(2)}) collective-permute-start(bf16[12,1,64,2,256]{4,2,0,3,1:T(8,128)(2,1)S(1)} %pad_maximum_fusion.2), channel_id=1, source_target_pairs={{2,0},{3,1},{6,4},{7,5},{10,8},{11,9},{14,12},{15,13},{18,16},{19,... | collective-permute-start | bytes 2359304 | tf_op jit(solution)/shard_map/ppermute | solution.py:18
  153.0 15.1 %copy-start.4 = (f32[4]{0:T(128)S(1)}, f32[4]{0:T(128)}, u32[]{:S(2)}) copy-start(f32[4]{0:T(128)} %param.13) | copy-start | bytes 52
  153.6 10.5 %collective-permute-start.12 = (bf16[4,1,64,2,256]{4,2,0,3,1:T(8,128)(2,1)S(1)}, bf16[4,1,64,2,256]{4,2,0,3,1:T(8,128)(2,1)S(1)}, u32[]{:S(2)}, u32[]{:S(2)}) collective-permute-start(bf16[4,1,64,2,256]{4,2,0,3,1:T(8,128)(2,1)S(1)} %fusion.4), channel_id=1, source_target_pairs={{0,4},{4,8},{8,12},{12,0},{1,5},{5,9},{9,13},{13,1},{2,6},{6,10},{... | collective-permute-start | bytes 786440 | tf_op jit(solution)/shard_map/ppermute | solution.py:17
  154.2 11.0 %collective-permute-start.13 = (bf16[4,1,64,2,256]{4,2,0,3,1:T(8,128)(2,1)S(1)}, bf16[4,1,64,2,256]{4,2,0,3,1:T(8,128)(2,1)S(1)}, u32[]{:S(2)}, u32[]{:S(2)}) collective-permute-start(bf16[4,1,64,2,256]{4,2,0,3,1:T(8,128)(2,1)S(1)} %fusion.4), channel_id=1, source_target_pairs={{4,0},{8,4},{12,8},{0,12},{5,1},{9,5},{13,9},{1,13},{6,2},{10,6},{... | collective-permute-start | bytes 786440 | tf_op jit(solution)/shard_map/ppermute | solution.py:18
  165.3 15.6 %collective-permute-start.14 = (bf16[12,1,64,2,256]{4,2,0,3,1:T(8,128)(2,1)S(1)}, bf16[12,1,64,2,256]{4,2,0,3,1:T(8,128)(2,1)S(1)}, u32[]{:S(2)}, u32[]{:S(2)}) collective-permute-start(bf16[12,1,64,2,256]{4,2,0,3,1:T(8,128)(2,1)S(1)} %pad_maximum_fusion.3), channel_id=1, source_target_pairs={{0,2},{1,3},{4,6},{5,7},{8,10},{9,11},{12,14},{13,15},{16,18},{17,... | collective-permute-start | bytes 2359304 | tf_op jit(solution)/shard_map/ppermute | solution.py:17
  166.8 18.3 %collective-permute-start.15 = (bf16[12,1,64,2,256]{4,2,0,3,1:T(8,128)(2,1)S(1)}, bf16[12,1,64,2,256]{4,2,0,3,1:T(8,128)(2,1)S(1)}, u32[]{:S(2)}, u32[]{:S(2)}) collective-permute-start(bf16[12,1,64,2,256]{4,2,0,3,1:T(8,128)(2,1)S(1)} %pad_maximum_fusion.3), channel_id=1, source_target_pairs={{2,0},{3,1},{6,4},{7,5},{10,8},{11,9},{14,12},{15,13},{18,16},{19,... | collective-permute-start | bytes 2359304 | tf_op jit(solution)/shard_map/ppermute | solution.py:18
  191.4 1.1 copy-start.2
  195.3 4.4 %copy-start.3 = (s32[4,1,64,256]{3,2,1,0:T(8,128)S(1)}, s32[4,1,64,256]{3,2,1,0:T(8,128)}, u32[]{:S(2)}) copy-start(s32[4,1,64,256]{3,2,1,0:T(8,128)} %param.15) | copy-start | bytes 786436
Sparse Core Ops, SparseCore 0:
  196.7 61.2 reduce-scatter.3
where the time goes:
time: 267 us
  waiting for transfers between devices  149 us (56%)
  starting transfers between devices  30 us (11%)
  matrix products  26.6 us (10%)
  blocking collectives  17.8 us (7%)
  local copies, waits for them, and re-layouts  16.5 us (6%)
  between operations  15 us (6%)
  other arithmetic  12.3 us (5%)
    ppermute x8, waiting for transfers between devices, padded(): before = lax.ppermute(last, axis, up)  83.2 us
    unnamed x2, waiting for transfers between devices  39.9 us
    dot_general x108, matrix products, apply_operator(): jnp.einsum('ctik,ctkn->ctin', part, piece, preferred_element_type=jnp.flo...  26.3 us
    ppermute x8, waiting for transfers between devices, padded(): after = lax.ppermute(initial, axis, down)  25.4 us
    psum x1, blocking collectives, body(): quadratic = lax.psum(local_quad, ('wire', 'xsec')) * scale  17.8 us
    ppermute x8, starting transfers between devices, padded(): after = lax.ppermute(initial, axis, down)  15.9 us
    ppermute x8, starting transfers between devices, padded(): before = lax.ppermute(last, axis, up)  14.1 us
    unnamed x19, local copies, waits for them, and re-layouts  7.16 us
  transfers between devices with their start and end apart: 17, of which 17 were waited for; matrix products, arithmetic and copies ran while one was open for 3% of the time, Pallas kernels for 0%

commit v1 on v0

v1 whole, which is shorter than its diff:
```python
import functools
import math

import jax
import jax.numpy as jnp
from jax import lax
from jax.experimental import pallas as pl
from jax.experimental.pallas import tpu as pltpu
from jax.sharding import PartitionSpec as P

REACH = 4
STEPS = 4
MESH = pl.DeviceIdType.MESH
F32 = jnp.float32
BF16 = jnp.bfloat16


def dot(a, b):
    return jnp.dot(a, b, preferred_element_type=F32)


def kernel(n_w, n_x, scale, blocks, pattern, cur, prev, acc_in, coefs, sketch, signs,
           newest, before, summed, gram, quad,
           h_own, h_out, h_in, field, halo, part_out, part_in, image,
           g_all, g_out, g_in, q_out, q_in,
           z_send, z_recv, x_send, x_recv, h_send, h_recv, g_send, g_recv, q_send, q_recv):
    cells, orbs, _ = blocks.shape
    streams = cur.shape[0]
    w, x = lax.axis_index("wire"), lax.axis_index("xsec")
    n_off = h_out.shape[0]
    others = [(a, b) for a in range(n_w) for b in range(n_x) if a or b]

    def other(a, b):
        return lax.rem(w + a, n_w), lax.rem(x + b, n_x)

    barrier = pltpu.get_barrier_semaphore()
    for a, b in others:
        ow, ox = other(a, b)
        pl.semaphore_signal(barrier, inc=1, device_id={"wire": ow, "xsec": ox}, device_id_type=MESH)
    pl.semaphore_wait(barrier, len(others))

    pending = []

    def send(src, dst, ssem, rsem, where):
        copy = pltpu.make_async_remote_copy(
            src_ref=src, dst_ref=dst, send_sem=ssem, recv_sem=rsem,
            device_id=where, device_id_type=MESH)
        copy.start()
        pending.append(copy)
        return copy

    right, left = lax.rem(w + 1, n_w), lax.rem(w + n_w - 1, n_w)

    def send_wire(s, k):
        src = cur.at[s] if k == 0 else field.at[k - 1, s]
        return [
            send(src, halo.at[k, s, 0], z_send.at[k, s, 0], z_recv.at[k, s, 0], {"wire": right}),
            send(src, halo.at[k, s, 1], z_send.at[k, s, 1], z_recv.at[k, s, 1], {"wire": left}),
        ]

    wires = {s: send_wire(s, 0) for s in range(streams)}

    if n_x == 1:
        weights = []
    elif n_x == 2:
        low = (x == 1).astype(F32)
        weights = [{0: low, 2: 1.0 - low}]
        to = [1 - x]
        back = [1 - x]
    else:
        weights = [{2: (x < n_x - 1).astype(F32)}, {0: (x > 0).astype(F32)}]
        to = [lax.rem(x + 1, n_x), lax.rem(x + n_x - 1, n_x)]
        back = [to[1], to[0]]

    def banded(c, part, weight):
        pieces = []
        for j in range(cells):
            d = part * cells + j - c
            if 0 <= d <= 2 * REACH:
                piece = None
                for e, factor in weight.items():
                    col = 3 * d + e
                    m = pattern[c, col].astype(F32)
                    if factor is not None:
                        m = m * factor
                    term = blocks[c, :, col * orbs:(col + 1) * orbs].astype(F32) * m
                    piece = term if piece is None else piece + term
                pieces.append(piece.astype(BF16))
            else:
                pieces.append(jnp.zeros((orbs, orbs), BF16))
        return jnp.concatenate(pieces, axis=1)

    rows = cells * orbs
    h_copies = {}
    for part in (1, 0, 2):
        for i, weight in enumerate(weights):
            for c in range(cells):
                h_out[i, part, c * orbs:(c + 1) * orbs, :] = banded(c, part, weight)
            h_copies[i, part] = send(h_out.at[i, part], h_in.at[i, part], h_send.at[i, part],
                                     h_recv.at[i, part], {"xsec": to[i]})
    for part in range(3):
        for c in range(cells):
            h_own[part, c * orbs:(c + 1) * orbs, :] = banded(c, part, {1: None})
    summed[...] = acc_in[...]
    for i in range(n_off):
        for part in range(3):
            h_copies[i, part].wait_recv()

    def apply(h, i, s, k):
        mine = cur[s] if k == 0 else field[k - 1, s]
        total = dot(h[i + (1,)], mine)
        total = total + dot(h[i + (0,)], halo[k, s, 0])
        return total + dot(h[i + (2,)], halo[k, s, 1])

    def step(s, k):
        for copy in wires[s]:
            copy.wait_recv()
        xs = []
        for i in range(n_off):
            part_out[k, s, i] = apply(h_in, (i,), s, k).astype(BF16)
            xs.append(send(part_out.at[k, s, i], part_in.at[k, s, i], x_send.at[k, s, i],
                           x_recv.at[k, s, i], {"xsec": back[i]}))
        image[s] = apply(h_own, (), s, k)
        for copy in xs:
            copy.wait_recv()
        total = image[s]
        for i in range(n_off):
            total = total + part_in[k, s, i].astype(F32)
        old = prev[s] if k == 0 else (cur[s] if k == 1 else field[k - 2, s])
        nxt = (2.0 * total - old.astype(F32)).astype(BF16)
        field[k, s] = nxt
        if k < STEPS - 1:
            wires[s] = send_wire(s, k + 1)
        summed[s] = summed[s] + coefs[k] * nxt.astype(F32)
        if k == STEPS - 1:
            newest[s] = nxt
        if k == STEPS - 2:
            before[s] = nxt

    half = streams // 2
    wide = cur.shape[2]
    receives = []
    mine = w * n_x + x

    def gram_part():
        for s in range(half):
            sketched = summed[s].astype(BF16)
            g = lax.dot_general(sketch[...], sketched, (((0,), (0,)), ((), ())),
                                preferred_element_type=F32)
            g = g.reshape(g_all.shape[0], g_all.shape[1], wide)
            g_all[:, :, s * wide:(s + 1) * wide] = g
            g_out[:, :, s * wide:(s + 1) * wide] = g.astype(BF16)
        for n, (a, b) in enumerate(others):
            ow, ox = other(a, b)
            receives.append(send(g_out.at[ow * n_x + ox], g_in.at[n], g_send.at[n], g_recv.at[n],
                                 {"wire": ow, "xsec": ox}))

    for k in range(STEPS):
        for s in range(streams):
            step(s, k)
            if k == STEPS - 1 and s == half - 1:
                gram_part()

    for s in range(half):
        at = slice(s * wide, (s + 1) * wide)
        pm = (2 * signs[:, at] - 1).astype(F32)
        q_out[:, at] = jnp.sum(pm * summed[half + s], axis=0, keepdims=True)
    q_copies = []
    for n, (a, b) in enumerate(others):
        ow, ox = other(a, b)
        q_copies.append(send(q_out, q_in.at[n], q_send.at[n], q_recv.at[n],
                             {"wire": ow, "xsec": ox}))
    for copy in receives:
        copy.wait_recv()
    total = g_all[mine]
    for n in range(len(others)):
        total = total + g_in[n].astype(F32)
    gram[...] = total * scale
    for copy in q_copies:
        copy.wait_recv()
    total = q_out[...]
    for n in range(len(others)):
        total = total + q_in[n]
    quad[...] = total * scale
    for copy in pending:
        copy.wait_send()


def body(n_w, n_x, blocks, pattern, current, previous, accum, coefs, sketch, signs):
    cells, tiles, orbs, wide = blocks.shape
    assert tiles == 1 and cells == REACH
    halves, cols = current.shape[3:]
    rows = cells * orbs
    streams = halves

    def split(a):
        return a.reshape(rows, halves, cols).transpose(1, 0, 2)

    def join(a):
        return a.transpose(1, 0, 2).reshape(cells, tiles, orbs, halves, cols)

    n_off = min(n_x - 1, 2)
    n_dev = n_w * n_x
    g_rows = sketch.shape[3] // n_dev
    scale = 1.0 / math.sqrt(rows * n_dev)
    vmem = pl.BlockSpec(memory_space=pltpu.VMEM)
    smem = pl.BlockSpec(memory_space=pltpu.SMEM)
    dma = pltpu.SemaphoreType.DMA
    S = jax.ShapeDtypeStruct
    out = pl.pallas_call(
        functools.partial(kernel, n_w, n_x, scale),
        out_shape=(
            S((streams, rows, cols), BF16),
            S((streams, rows, cols), BF16),
            S((streams, rows, cols), F32),
            S((g_rows, cols), F32),
            S((1, cols), F32),
        ),
        in_specs=[vmem, smem, vmem, vmem, vmem, smem, vmem, vmem],
        out_specs=(vmem,) * 5,
        scratch_shapes=[
            pltpu.VMEM((3, rows, rows), BF16),
            pltpu.VMEM((n_off, 3, rows, rows), BF16),
            pltpu.VMEM((n_off, 3, rows, rows), BF16),
            pltpu.VMEM((STEPS, streams, rows, cols), BF16),
            pltpu.VMEM((STEPS, streams, 2, rows, cols), BF16),
            pltpu.VMEM((STEPS, streams, n_off, rows, cols), BF16),
            pltpu.VMEM((STEPS, streams, n_off, rows, cols), BF16),
            pltpu.VMEM((streams, rows, cols), F32),
            pltpu.VMEM((n_dev, g_rows, cols), F32),
            pltpu.VMEM((n_dev, g_rows, cols), BF16),
            pltpu.VMEM((n_dev - 1, g_rows, cols), BF16),
            pltpu.VMEM((1, cols), F32),
            pltpu.VMEM((n_dev - 1, 1, cols), F32),
            dma((STEPS, streams, 2)),
            dma((STEPS, streams, 2)),
            dma((STEPS, streams, n_off)),
            dma((STEPS, streams, n_off)),
            dma((n_off, 3)),
            dma((n_off, 3)),
            dma((n_dev - 1,)),
            dma((n_dev - 1,)),
            dma((n_dev - 1,)),
            dma((n_dev - 1,)),
        ],
        compiler_params=pltpu.CompilerParams(
            collective_id=0, has_side_effects=True, vmem_limit_bytes=40 * 1024 * 1024),
    )(
        blocks.reshape(cells, orbs, wide), pattern.reshape(cells, -1), split(current),
        split(previous), split(accum), coefs, sketch.reshape(rows, -1), signs.reshape(rows, cols))
    newest, before, summed, gram, quad = out
    return join(newest), join(before), join(summed), gram, quad.reshape(cols)


def solution(mesh):
    return jax.shard_map(
        functools.partial(body, mesh.shape["wire"], mesh.shape["xsec"]),
        mesh=mesh,
        in_specs=(
            P(("sample", "wire"), "xsec", None, None),
            P(("sample", "wire"), "xsec", None),
            P(("sample", "wire"), "xsec", None, None, "cols"),
            P(("sample", "wire"), "xsec", None, None, "cols"),
            P(("sample", "wire"), "xsec", None, None, "cols"),
            P(),
            P(("sample", "wire"), "xsec", None, None),
            P(("sample", "wire"), "xsec", None, "cols"),
        ),
        out_specs=(
            P(("sample", "wire"), "xsec", None, None, "cols"),
            P(("sample", "wire"), "xsec", None, None, "cols"),
            P(("sample", "wire"), "xsec", None, None, "cols"),
            P(("sample", "wire", "xsec"), "cols"),
            P(("sample", "cols")),
        ),
        check_vma=False,
    )
```

time: 267 us -> 79 us (0.30)
  waiting for transfers between devices: 149 us -> 0 us
  Pallas kernels: 0 us -> 70.7 us
  starting transfers between devices: 30 us -> 0 us
  matrix products: 26.6 us -> 0 us
  blocking collectives: 17.8 us -> 0 us
  between operations: 15 us -> 0.72 us
  other arithmetic: 12.3 us -> 0 us
  local copies, waits for them, and re-layouts: 16.5 us -> 7.48 us
    ppermute x16 -> x0, waiting for transfers between devices: 109 us -> none  [the longest x8 83.2 us: padded(): before = lax.ppermute(last, axis, up)]
    pallas_call x0 -> x1, Pallas kernels: none -> 70.7 us  [body(): pl.pallas_call(functools.partial(kernel, n_w, n_x, scale), out_shape=(S((...]
    unnamed x2 -> x0, waiting for transfers between devices: 39.9 us -> none
    ppermute x16 -> x0, starting transfers between devices: 29.9 us -> none  [the longest x8 15.9 us: padded(): after = lax.ppermute(initial, axis, down)]
    dot_general x109 -> x0, matrix products: 26.6 us -> none  [the longest x108 26.3 us: apply_operator(): jnp.einsum('ctik,ctkn->ctin', part, piece, preferred_element_type=jnp.flo...]
    psum x1 -> x0, blocking collectives: 17.8 us -> none  [body(): quadratic = lax.psum(local_quad, ('wire', 'xsec')) * scale]
    reshape x4 -> x0, local copies, waits for them, and re-layouts: 5.95 us -> none  [apply_operator(): extended.reshape(cells + 2 * reach, tiles + 2, orbs, halves * local_cols)]
    concatenate x4 -> x0, other arithmetic: 4.84 us -> none  [padded(): x = jnp.concatenate([before, x, after], axis=dim)]
  transfers between devices with their start and end apart: 17 -> 0, of which waited for: 17 -> 0; matrix products, arithmetic and copies ran while one was open for 3% -> 0% of each run, Pallas kernels for 0% -> 0%
where the time goes in v1:
time: 79 us; the launch traced here: 78.9 us
  Pallas kernels  70.7 us (89%)
  local copies, waits for them, and re-layouts  7.48 us (9%)
    pallas_call x1, Pallas kernels, body(): pl.pallas_call(functools.partial(kernel, n_w, n_x, scale), out_shape=(S((...  70.7 us
    unnamed x20, local copies, waits for them, and re-layouts  7.48 us

profile of v1, /device:TPU:0, one launch (start us, length us, event | category | flops | bytes accessed | tf_op | source)
XLA Modules:
  0.0 78.9 jit_solution(12489674342160586564)
XLA Ops:
  0.6 0.0 copy-start.5
  0.6 1.0 %copy.13 = bf16[4,1,64,2,256]{4,2,0,3,1:T(8,128)(2,1)S(1)} copy(bf16[4,1,64,2,256]{4,3,2,1,0:T(2,128)(2,1)} %param.10) | data formatting | bytes 524288 | tf_op args[2]
  1.7 0.0 copy-start
  1.7 1.1 %copy.14 = bf16[4,1,64,2,256]{4,2,0,3,1:T(8,128)(2,1)S(1)} copy(bf16[4,1,64,2,256]{4,3,2,1,0:T(2,128)(2,1)} %param.11) | data formatting | bytes 524288 | tf_op args[3]
  2.8 0.0 copy-done.5
  2.8 0.0 copy-start.1
  2.8 0.0 copy-start.2
  2.8 0.0 copy-start.3
  2.9 0.0 copy-start.4
  2.9 0.1 copy-done
  3.0 0.8 %copy-done.1 = bf16[4,1,64,512]{3,2,1,0:T(8,128)(2,1)S(1)} copy-done((bf16[4,1,64,512]{3,2,1,0:T(8,128)(2,1)S(1)}, bf16[4,1,64,512]{3,2,1,0:T(8,128)(2,1)}, u32[]{:S(2)}) %copy-start.1) | copy-done | bytes 262168
  3.8 0.1 copy-done.2
  3.8 0.0 copy-done.3
  3.8 0.0 copy-done.4
  3.8 70.7 %shard_map.119 = (bf16[2,256,256]{2,1,0:T(8,128)(2,1)S(1)}, bf16[2,256,256]{2,1,0:T(8,128)(2,1)S(1)}, f32[2,256,256]{2,1,0:T(8,128)S(1)}, f32[64,256]{1,0:T(8,128)S(1)}, f32[1,256]{1,0:T(1,128)S(1)}) custom-call(bf16[4,64,1728]{2,1,0:T(8,128)(2,1)S(1)} %bitcast.26, s32[4,27]{1,0:T(4,128)S(1)} %bitcast.32, bf16[2,256,256]{2,1,0:T(8,128)(2,1)S(1)} %bitcast.24, ...), custom_call_target="tpu_custom_call" | custom-call | tf_op jit(solution)/shard_map/pallas_call | solution.py:210
  74.5 1.0 %copy.16 = bf16[4,1,64,2,256]{4,3,2,1,0:T(2,128)(2,1)} copy(bf16[4,1,64,2,256]{4,2,0,3,1:T(8,128)(2,1)S(1)} %bitcast.31) | data formatting | bytes 524288
  75.5 1.0 %copy.17 = bf16[4,1,64,2,256]{4,3,2,1,0:T(2,128)(2,1)} copy(bf16[4,1,64,2,256]{4,2,0,3,1:T(8,128)(2,1)S(1)} %bitcast.30) | data formatting | bytes 524288
  76.5 1.2 %copy.18 = f32[4,1,64,2,256]{4,3,2,1,0:T(2,128)} copy(f32[4,1,64,2,256]{4,2,0,3,1:T(8,128)S(1)} %bitcast.27) | data formatting | bytes 1048576
  77.7 0.6 copy.21
  78.3 0.6 copy.22
  (1 shorter events, 0.0 us)
Async XLA Ops:
  0.6 2.1 %copy-start.5 = (f32[4,1,64,2,256]{4,3,2,1,0:T(2,128)S(1)}, f32[4,1,64,2,256]{4,3,2,1,0:T(2,128)}, u32[]{:S(2)}) copy-start(f32[4,1,64,2,256]{4,3,2,1,0:T(2,128)} %param.12) | copy-start | bytes 1572868
  1.7 1.3 %copy-start = (bf16[4,1,64,1728]{3,2,1,0:T(8,128)(2,1)S(1)}, bf16[4,1,64,1728]{3,2,1,0:T(8,128)(2,1)}, u32[]{:S(2)}) copy-start(bf16[4,1,64,1728]{3,2,1,0:T(8,128)(2,1)} %param.8) | copy-start | bytes 2654212
  2.8 1.0 %copy-start.1 = (bf16[4,1,64,512]{3,2,1,0:T(8,128)(2,1)S(1)}, bf16[4,1,64,512]{3,2,1,0:T(8,128)(2,1)}, u32[]{:S(2)}) copy-start(bf16[4,1,64,512]{3,2,1,0:T(8,128)(2,1)} %param.14) | copy-start | bytes 786436
  2.8 1.1 %copy-start.2 = (s32[4,1,64,256]{3,2,1,0:T(8,128)S(1)}, s32[4,1,64,256]{3,2,1,0:T(8,128)}, u32[]{:S(2)}) copy-start(s32[4,1,64,256]{3,2,1,0:T(8,128)} %param.15) | copy-start | bytes 786436
  2.8 1.1 %copy-start.3 = (s32[4,1,27]{2,1,0:T(1,128)S(1)}, s32[4,1,27]{2,1,0:T(1,128)}, u32[]{:S(2)}) copy-start(s32[4,1,27]{2,1,0:T(1,128)} %param.9) | copy-start | bytes 1300
  2.9 1.0 %copy-start.4 = (f32[4]{0:T(128)S(1)}, f32[4]{0:T(128)}, u32[]{:S(2)}) copy-start(f32[4]{0:T(128)} %coefs.1) | copy-start | bytes 52

commit v2 on v1

--- a/solution.py
+++ b/solution.py
@@ -19,13 +19,20 @@
     return jnp.dot(a, b, preferred_element_type=F32)
 
 
-def kernel(n_w, n_x, scale, blocks, pattern, cur, prev, acc_in, coefs, sketch, signs,
+def kernel(n_w, n_x, n_c, scale, blocks, pattern, cur, prev, acc_in, coefs, sketch, signs,
            newest, before, summed, gram, quad,
            h_own, h_out, h_in, field, halo, part_out, part_in, image,
            g_all, g_out, g_in, q_out, q_in,
-           z_send, z_recv, x_send, x_recv, h_send, h_recv, g_send, g_recv, q_send, q_recv):
+           z_send, z_recv, x_send, x_recv, h_send, h_recv, c_send, c_recv, g_send, g_recv,
+           q_send, q_recv):
     cells, orbs, _ = blocks.shape
-    streams = cur.shape[0]
+    halves, _, cols = cur.shape
+    streams, wide = field.shape[1], field.shape[3]
+    half = streams // halves
+
+    def view(ref, s):
+        return ref.at[s // half, :, pl.ds(s % half * wide, wide)]
+
     w, x = lax.axis_index("wire"), lax.axis_index("xsec")
     n_off = h_out.shape[0]
     others = [(a, b) for a in range(n_w) for b in range(n_x) if a or b]
@@ -37,7 +44,11 @@
     for a, b in others:
         ow, ox = other(a, b)
         pl.semaphore_signal(barrier, inc=1, device_id={"wire": ow, "xsec": ox}, device_id_type=MESH)
-    pl.semaphore_wait(barrier, len(others))
+    core = lax.axis_index("cols")
+    for a in range(1, n_c):
+        pl.semaphore_signal(barrier, inc=1, device_id={"cols": lax.rem(core + a, n_c)},
+                            device_id_type=MESH)
+    pl.semaphore_wait(barrier, len(others) + n_c - 1)
 
     pending = []
 
@@ -52,7 +63,7 @@
     right, left = lax.rem(w + 1, n_w), lax.rem(w + n_w - 1, n_w)
 
     def send_wire(s, k):
-        src = cur.at[s] if k == 0 else field.at[k - 1, s]
+        src = view(cur, s) if k == 0 else field.at[k - 1, s]
         return [
             send(src, halo.at[k, s, 0], z_send.at[k, s, 0], z_recv.at[k, s, 0], {"wire": right}),
             send(src, halo.at[k, s, 1], z_send.at[k, s, 1], z_recv.at[k, s, 1], {"wire": left}),
@@ -91,60 +102,78 @@
         return jnp.concatenate(pieces, axis=1)
 
     rows = cells * orbs
-    h_copies = {}
+    share = rows // n_c
+    own_share = pl.ds(pl.multiple_of(core * share, share), share)
+    h_copies = []
     for part in (1, 0, 2):
         for i, weight in enumerate(weights):
             for c in range(cells):
                 h_out[i, part, c * orbs:(c + 1) * orbs, :] = banded(c, part, weight)
-            h_copies[i, part] = send(h_out.at[i, part], h_in.at[i, part], h_send.at[i, part],
-                                     h_recv.at[i, part], {"xsec": to[i]})
+            h_copies.append((i, part, send(
+                h_out.at[i, part, own_share], h_in.at[i, part, own_share],
+                h_send.at[i, part], h_recv.at[i, part], {"xsec": to[i]})))
     for part in range(3):
         for c in range(cells):
             h_own[part, c * orbs:(c + 1) * orbs, :] = banded(c, part, {1: None})
+    c_copies = []
+    for i, part, copy in h_copies:
+        copy.wait_recv()
+        for a in range(1, n_c):
+            c_copies.append(send(
+                h_in.at[i, part, own_share], h_in.at[i, part, own_share],
+                c_send.at[i, part, a - 1], c_recv.at[i, part, a - 1],
+                {"cols": lax.rem(core + a, n_c)}))
     summed[...] = acc_in[...]
-    for i in range(n_off):
-        for part in range(3):
-            h_copies[i, part].wait_recv()
+    for copy in c_copies:
+        copy.wait_recv()
 
     def apply(h, i, s, k):
-        mine = cur[s] if k == 0 else field[k - 1, s]
+        mine = view(cur, s)[...] if k == 0 else field[k - 1, s]
         total = dot(h[i + (1,)], mine)
         total = total + dot(h[i + (0,)], halo[k, s, 0])
         return total + dot(h[i + (2,)], halo[k, s, 1])
 
-    def step(s, k):
+    partials = {}
+
+    def multiply(k, s):
         for copy in wires[s]:
             copy.wait_recv()
-        xs = []
+        partials[s] = []
         for i in range(n_off):
             part_out[k, s, i] = apply(h_in, (i,), s, k).astype(BF16)
-            xs.append(send(part_out.at[k, s, i], part_in.at[k, s, i], x_send.at[k, s, i],
-                           x_recv.at[k, s, i], {"xsec": back[i]}))
+            partials[s].append(send(
+                part_out.at[k, s, i], part_in.at[k, s, i], x_send.at[k, s, i],
+                x_recv.at[k, s, i], {"xsec": back[i]}))
         image[s] = apply(h_own, (), s, k)
-        for copy in xs:
+
+    def advance(k, s):
+        for copy in partials[s]:
             copy.wait_recv()
         total = image[s]
         for i in range(n_off):
             total = total + part_in[k, s, i].astype(F32)
-        old = prev[s] if k == 0 else (cur[s] if k == 1 else field[k - 2, s])
+        old = view((prev, cur)[k], s)[...] if k < 2 else field[k - 2, s]
         nxt = (2.0 * total - old.astype(F32)).astype(BF16)
         field[k, s] = nxt
         if k < STEPS - 1:
             wires[s] = send_wire(s, k + 1)
-        summed[s] = summed[s] + coefs[k] * nxt.astype(F32)
+        acc = view(summed, s)
+        acc[...] = acc[...] + coefs[k] * nxt.astype(F32)
         if k == STEPS - 1:
-            newest[s] = nxt
+            view(newest, s)[...] = nxt
+            if s == half - 1:
+                gram_part()
+            if s >= half:
+                quad_part(s - half)
         if k == STEPS - 2:
-            before[s] = nxt
-
-    half = streams // 2
-    wide = cur.shape[2]
+            view(before, s)[...] = nxt
+
     receives = []
     mine = w * n_x + x
 
     def gram_part():
         for s in range(half):
-            sketched = summed[s].astype(BF16)
+            sketched = view(summed, s)[...].astype(BF16)
             g = lax.dot_general(sketch[...], sketched, (((0,), (0,)), ((), ())),
                                 preferred_element_type=F32)
             g = g.reshape(g_all.shape[0], g_all.shape[1], wide)
@@ -155,16 +184,20 @@
             receives.append(send(g_out.at[ow * n_x + ox], g_in.at[n], g_send.at[n], g_recv.at[n],
                                  {"wire": ow, "xsec": ox}))
 
+    def quad_part(s):
+        at = slice(s * wide, (s + 1) * wide)
+        pm = (2 * signs[:, at] - 1).astype(F32)
+        q_out[:, at] = jnp.sum(pm * view(summed, half + s)[...], axis=0, keepdims=True)
+
+    last = None
     for k in range(STEPS):
         for s in range(streams):
-            step(s, k)
-            if k == STEPS - 1 and s == half - 1:
-                gram_part()
-
-    for s in range(half):
-        at = slice(s * wide, (s + 1) * wide)
-        pm = (2 * signs[:, at] - 1).astype(F32)
-        q_out[:, at] = jnp.sum(pm * summed[half + s], axis=0, keepdims=True)
+            multiply(k, s)
+            if last is not None:
+                advance(*last)
+            last = (k, s)
+    advance(*last)
+
     q_copies = []
     for n, (a, b) in enumerate(others):
         ow, ox = other(a, b)
@@ -186,12 +219,13 @@
         copy.wait_send()
 
 
-def body(n_w, n_x, blocks, pattern, current, previous, accum, coefs, sketch, signs):
+def body(n_w, n_x, n_c, blocks, pattern, current, previous, accum, coefs, sketch, signs):
     cells, tiles, orbs, wide = blocks.shape
     assert tiles == 1 and cells == REACH
     halves, cols = current.shape[3:]
     rows = cells * orbs
-    streams = halves
+    lanes = 128 if cols % 128 == 0 else cols
+    streams = halves * (cols // lanes)
 
     def split(a):
         return a.reshape(rows, halves, cols).transpose(1, 0, 2)
@@ -208,11 +242,11 @@
     dma = pltpu.SemaphoreType.DMA
     S = jax.ShapeDtypeStruct
     out = pl.pallas_call(
-        functools.partial(kernel, n_w, n_x, scale),
+        functools.partial(kernel, n_w, n_x, n_c, scale),
         out_shape=(
-            S((streams, rows, cols), BF16),
-            S((streams, rows, cols), BF16),
-            S((streams, rows, cols), F32),
+            S((halves, rows, cols), BF16),
+            S((halves, rows, cols), BF16),
+            S((halves, rows, cols), F32),
             S((g_rows, cols), F32),
             S((1, cols), F32),
         ),
@@ -222,11 +256,11 @@
             pltpu.VMEM((3, rows, rows), BF16),
             pltpu.VMEM((n_off, 3, rows, rows), BF16),
             pltpu.VMEM((n_off, 3, rows, rows), BF16),
-            pltpu.VMEM((STEPS, streams, rows, cols), BF16),
-            pltpu.VMEM((STEPS, streams, 2, rows, cols), BF16),
-            pltpu.VMEM((STEPS, streams, n_off, rows, cols), BF16),
-            pltpu.VMEM((STEPS, streams, n_off, rows, cols), BF16),
-            pltpu.VMEM((streams, rows, cols), F32),
+            pltpu.VMEM((STEPS, streams, rows, lanes), BF16),
+            pltpu.VMEM((STEPS, streams, 2, rows, lanes), BF16),
+            pltpu.VMEM((STEPS, streams, n_off, rows, lanes), BF16),
+            pltpu.VMEM((STEPS, streams, n_off, rows, lanes), BF16),
+            pltpu.VMEM((streams, rows, lanes), F32),
             pltpu.VMEM((n_dev, g_rows, cols), F32),
             pltpu.VMEM((n_dev, g_rows, cols), BF16),
             pltpu.VMEM((n_dev - 1, g_rows, cols), BF16),
@@ -238,6 +272,8 @@
             dma((STEPS, streams, n_off)),
             dma((n_off, 3)),
             dma((n_off, 3)),
+            dma((n_off, 3, n_c)),
+            dma((n_off, 3, n_c)),
             dma((n_dev - 1,)),
             dma((n_dev - 1,)),
             dma((n_dev - 1,)),
@@ -254,7 +290,7 @@
 
 def solution(mesh):
     return jax.shard_map(
-        functools.partial(body, mesh.shape["wire"], mesh.shape["xsec"]),
+        functools.partial(body, mesh.shape["wire"], mesh.shape["xsec"], mesh.shape["cols"]),
         mesh=mesh,
         in_specs=(
             P(("sample", "wire"), "xsec", None, None),

time: 79 us -> 71.7 us (0.908)
  Pallas kernels: 70.7 us -> 63.3 us
    pallas_call x1, Pallas kernels: 70.7 us -> 63.3 us  [body(): pl.pallas_call(functools.partial(kernel, n_w, n_x, n_c, scale), out_shape...]
where the time goes in v2:
time: 71.7 us; the launch traced here: 71.5 us
  Pallas kernels  63.3 us (88%)
  local copies, waits for them, and re-layouts  7.48 us (10%)
  between operations  0.72 us (1%)
    pallas_call x1, Pallas kernels, body(): pl.pallas_call(functools.partial(kernel, n_w, n_x, n_c, scale), out_shape...  63.3 us
    unnamed x20, local copies, waits for them, and re-layouts  7.48 us

profile of v2, /device:TPU:0, one launch (start us, length us, event | category | flops | bytes accessed | tf_op | source)
XLA Modules:
  0.0 71.5 jit_solution(12046706155737213254)
XLA Ops:
  0.6 0.0 copy-start.5
  0.6 1.0 %copy.13 = bf16[4,1,64,2,256]{4,2,0,3,1:T(8,128)(2,1)S(1)} copy(bf16[4,1,64,2,256]{4,3,2,1,0:T(2,128)(2,1)} %param.10) | data formatting | bytes 524288 | tf_op args[2]
  1.7 0.0 copy-start
  1.7 1.1 %copy.14 = bf16[4,1,64,2,256]{4,2,0,3,1:T(8,128)(2,1)S(1)} copy(bf16[4,1,64,2,256]{4,3,2,1,0:T(2,128)(2,1)} %param.11) | data formatting | bytes 524288 | tf_op args[3]
  2.8 0.0 copy-done.5
  2.8 0.0 copy-start.1
  2.8 0.0 copy-start.2
  2.8 0.0 copy-start.3
  2.9 0.0 copy-start.4
  2.9 0.1 copy-done
  3.0 0.8 %copy-done.1 = bf16[4,1,64,512]{3,2,1,0:T(8,128)(2,1)S(1)} copy-done((bf16[4,1,64,512]{3,2,1,0:T(8,128)(2,1)S(1)}, bf16[4,1,64,512]{3,2,1,0:T(8,128)(2,1)}, u32[]{:S(2)}) %copy-start.1) | copy-done | bytes 262168
  3.8 0.1 copy-done.2
  3.8 0.0 copy-done.3
  3.8 0.0 copy-done.4
  3.8 63.3 %shard_map.119 = (bf16[2,256,256]{2,1,0:T(8,128)(2,1)S(1)}, bf16[2,256,256]{2,1,0:T(8,128)(2,1)S(1)}, f32[2,256,256]{2,1,0:T(8,128)S(1)}, f32[64,256]{1,0:T(8,128)S(1)}, f32[1,256]{1,0:T(1,128)S(1)}) custom-call(bf16[4,64,1728]{2,1,0:T(8,128)(2,1)S(1)} %bitcast.26, s32[4,27]{1,0:T(4,128)S(1)} %bitcast.32, bf16[2,256,256]{2,1,0:T(8,128)(2,1)S(1)} %bitcast.24, ...), custom_call_target="tpu_custom_call" | custom-call | tf_op jit(solution)/shard_map/pallas_call | solution.py:244
  67.1 1.0 %copy.16 = bf16[4,1,64,2,256]{4,3,2,1,0:T(2,128)(2,1)} copy(bf16[4,1,64,2,256]{4,2,0,3,1:T(8,128)(2,1)S(1)} %bitcast.31) | data formatting | bytes 524288
  68.1 1.0 %copy.17 = bf16[4,1,64,2,256]{4,3,2,1,0:T(2,128)(2,1)} copy(bf16[4,1,64,2,256]{4,2,0,3,1:T(8,128)(2,1)S(1)} %bitcast.30) | data formatting | bytes 524288
  69.1 1.2 %copy.18 = f32[4,1,64,2,256]{4,3,2,1,0:T(2,128)} copy(f32[4,1,64,2,256]{4,2,0,3,1:T(8,128)S(1)} %bitcast.27) | data formatting | bytes 1048576
  70.3 0.6 copy.21
  70.9 0.6 copy.22
  (1 shorter events, 0.0 us)
Async XLA Ops:
  0.6 2.1 %copy-start.5 = (f32[4,1,64,2,256]{4,3,2,1,0:T(2,128)S(1)}, f32[4,1,64,2,256]{4,3,2,1,0:T(2,128)}, u32[]{:S(2)}) copy-start(f32[4,1,64,2,256]{4,3,2,1,0:T(2,128)} %param.12) | copy-start | bytes 1572868
  1.7 1.3 %copy-start = (bf16[4,1,64,1728]{3,2,1,0:T(8,128)(2,1)S(1)}, bf16[4,1,64,1728]{3,2,1,0:T(8,128)(2,1)}, u32[]{:S(2)}) copy-start(bf16[4,1,64,1728]{3,2,1,0:T(8,128)(2,1)} %param.8) | copy-start | bytes 2654212
  2.8 1.0 %copy-start.1 = (bf16[4,1,64,512]{3,2,1,0:T(8,128)(2,1)S(1)}, bf16[4,1,64,512]{3,2,1,0:T(8,128)(2,1)}, u32[]{:S(2)}) copy-start(bf16[4,1,64,512]{3,2,1,0:T(8,128)(2,1)} %param.14) | copy-start | bytes 786436
  2.8 1.1 %copy-start.2 = (s32[4,1,64,256]{3,2,1,0:T(8,128)S(1)}, s32[4,1,64,256]{3,2,1,0:T(8,128)}, u32[]{:S(2)}) copy-start(s32[4,1,64,256]{3,2,1,0:T(8,128)} %param.15) | copy-start | bytes 786436
  2.8 1.1 %copy-start.3 = (s32[4,1,27]{2,1,0:T(1,128)S(1)}, s32[4,1,27]{2,1,0:T(1,128)}, u32[]{:S(2)}) copy-start(s32[4,1,27]{2,1,0:T(1,128)} %param.9) | copy-start | bytes 1300
  2.9 1.0 %copy-start.4 = (f32[4]{0:T(128)S(1)}, f32[4]{0:T(128)}, u32[]{:S(2)}) copy-start(f32[4]{0:T(128)} %coefs.1) | copy-start | bytes 52

commit v3 on v2

--- a/solution.py
+++ b/solution.py
@@ -19,12 +19,12 @@
     return jnp.dot(a, b, preferred_element_type=F32)
 
 
-def kernel(n_w, n_x, n_c, scale, blocks, pattern, cur, prev, acc_in, coefs, sketch, signs,
+def kernel(n_w, n_x, n_c, scale, blocks, pattern, cur, prev, acc_in, coefs, sketch_hbm, signs_hbm,
            newest, before, summed, gram, quad,
            h_own, h_out, h_in, field, halo, part_out, part_in, image,
            g_all, g_out, g_in, q_out, q_in,
            z_send, z_recv, x_send, x_recv, h_send, h_recv, c_send, c_recv, g_send, g_recv,
-           q_send, q_recv):
+           q_send, q_recv, sketch, signs, load):
     cells, orbs, _ = blocks.shape
     halves, _, cols = cur.shape
     streams, wide = field.shape[1], field.shape[3]
@@ -50,6 +50,8 @@
                             device_id_type=MESH)
     pl.semaphore_wait(barrier, len(others) + n_c - 1)
 
+    loads = [pltpu.make_async_copy(sketch_hbm, sketch, load.at[0]),
+             pltpu.make_async_copy(signs_hbm, signs, load.at[1])]
     pending = []
 
     def send(src, dst, ssem, rsem, where):
@@ -70,6 +72,9 @@
         ]
 
     wires = {s: send_wire(s, 0) for s in range(streams)}
+
+    for copy in loads:
+        copy.start()
 
     if n_x == 1:
         weights = []
@@ -124,27 +129,27 @@
                 c_send.at[i, part, a - 1], c_recv.at[i, part, a - 1],
                 {"cols": lax.rem(core + a, n_c)}))
     summed[...] = acc_in[...]
+    for copy in loads:
+        copy.wait()
     for copy in c_copies:
         copy.wait_recv()
 
-    def apply(h, i, s, k):
+    partials = {}
+
+    def multiply(k, s):
         mine = view(cur, s)[...] if k == 0 else field[k - 1, s]
-        total = dot(h[i + (1,)], mine)
-        total = total + dot(h[i + (0,)], halo[k, s, 0])
-        return total + dot(h[i + (2,)], halo[k, s, 1])
-
-    partials = {}
-
-    def multiply(k, s):
-        for copy in wires[s]:
+        image[s] = dot(h_own[1], mine)
+        sums = [dot(h_in[i, 1], mine) for i in range(n_off)]
+        for side, copy in enumerate(wires[s]):
             copy.wait_recv()
+            sums = [total + dot(h_in[i, 2 * side], halo[k, s, side]) for i, total in enumerate(sums)]
         partials[s] = []
         for i in range(n_off):
-            part_out[k, s, i] = apply(h_in, (i,), s, k).astype(BF16)
+            part_out[k, s, i] = sums[i].astype(BF16)
             partials[s].append(send(
                 part_out.at[k, s, i], part_in.at[k, s, i], x_send.at[k, s, i],
                 x_recv.at[k, s, i], {"xsec": back[i]}))
-        image[s] = apply(h_own, (), s, k)
+        image[s] = image[s] + (dot(h_own[0], halo[k, s, 0]) + dot(h_own[2], halo[k, s, 1]))
 
     def advance(k, s):
         for copy in partials[s]:
@@ -238,6 +243,7 @@
     g_rows = sketch.shape[3] // n_dev
     scale = 1.0 / math.sqrt(rows * n_dev)
     vmem = pl.BlockSpec(memory_space=pltpu.VMEM)
+    hbm = pl.BlockSpec(memory_space=pltpu.HBM)
     smem = pl.BlockSpec(memory_space=pltpu.SMEM)
     dma = pltpu.SemaphoreType.DMA
     S = jax.ShapeDtypeStruct
@@ -250,7 +256,7 @@
             S((g_rows, cols), F32),
             S((1, cols), F32),
         ),
-        in_specs=[vmem, smem, vmem, vmem, vmem, smem, vmem, vmem],
+        in_specs=[vmem, smem, vmem, vmem, vmem, smem, hbm, hbm],
         out_specs=(vmem,) * 5,
         scratch_shapes=[
             pltpu.VMEM((3, rows, rows), BF16),
@@ -278,6 +284,9 @@
             dma((n_dev - 1,)),
             dma((n_dev - 1,)),
             dma((n_dev - 1,)),
+            pltpu.VMEM((rows, sketch.shape[3]), BF16),
+            pltpu.VMEM((rows, cols), jnp.int32),
+            dma((2,)),
         ],
         compiler_params=pltpu.CompilerParams(
             collective_id=0, has_side_effects=True, vmem_limit_bytes=40 * 1024 * 1024),

time: 71.7 us -> 72.1 us (level)
  no operation moved by 1% of the time
where the time goes in v3:
time: 72.1 us; the launch traced here: 71.9 us
  Pallas kernels  63.7 us (88%)
  local copies, waits for them, and re-layouts  7.48 us (10%)
    pallas_call x1, Pallas kernels, body(): pl.pallas_call(functools.partial(kernel, n_w, n_x, n_c, scale), out_shape...  63.7 us
    unnamed x20, local copies, waits for them, and re-layouts  7.48 us

profile of v3, /device:TPU:0, one launch (start us, length us, event | category | flops | bytes accessed | tf_op | source)
XLA Modules:
  0.0 71.9 jit_solution(12363467871425913552)
XLA Ops:
  0.6 0.0 copy-start.5
  0.6 1.0 %copy.13 = bf16[4,1,64,2,256]{4,2,0,3,1:T(8,128)(2,1)S(1)} copy(bf16[4,1,64,2,256]{4,3,2,1,0:T(2,128)(2,1)} %param.10) | data formatting | bytes 524288 | tf_op args[2]
  1.7 0.0 copy-start
  1.7 1.1 %copy.14 = bf16[4,1,64,2,256]{4,2,0,3,1:T(8,128)(2,1)S(1)} copy(bf16[4,1,64,2,256]{4,3,2,1,0:T(2,128)(2,1)} %param.11) | data formatting | bytes 524288 | tf_op args[3]
  2.8 0.0 copy-done.5
  2.8 0.0 copy-start.1
  2.8 0.0 copy-start.2
  2.8 0.0 copy-start.3
  2.9 0.0 copy-start.4
  2.9 0.1 copy-done
  3.0 0.8 %copy-done.1 = bf16[4,1,64,512]{3,2,1,0:T(8,128)(2,1)S(1)} copy-done((bf16[4,1,64,512]{3,2,1,0:T(8,128)(2,1)S(1)}, bf16[4,1,64,512]{3,2,1,0:T(8,128)(2,1)}, u32[]{:S(2)}) %copy-start.1) | copy-done | bytes 262168
  3.8 0.1 copy-done.2
  3.8 0.0 copy-done.3
  3.8 0.0 copy-done.4
  3.8 63.7 %shard_map.119 = (bf16[2,256,256]{2,1,0:T(8,128)(2,1)S(1)}, bf16[2,256,256]{2,1,0:T(8,128)(2,1)S(1)}, f32[2,256,256]{2,1,0:T(8,128)S(1)}, f32[64,256]{1,0:T(8,128)S(1)}, f32[1,256]{1,0:T(1,128)S(1)}) custom-call(bf16[4,64,1728]{2,1,0:T(8,128)(2,1)S(1)} %bitcast.26, s32[4,27]{1,0:T(4,128)S(1)} %bitcast.32, bf16[2,256,256]{2,1,0:T(8,128)(2,1)S(1)} %bitcast.24, ...), custom_call_target="tpu_custom_call" | custom-call | tf_op jit(solution)/shard_map/pallas_call | solution.py:250
  67.6 1.0 %copy.16 = bf16[4,1,64,2,256]{4,3,2,1,0:T(2,128)(2,1)} copy(bf16[4,1,64,2,256]{4,2,0,3,1:T(8,128)(2,1)S(1)} %bitcast.31) | data formatting | bytes 524288
  68.5 1.0 %copy.17 = bf16[4,1,64,2,256]{4,3,2,1,0:T(2,128)(2,1)} copy(bf16[4,1,64,2,256]{4,2,0,3,1:T(8,128)(2,1)S(1)} %bitcast.30) | data formatting | bytes 524288
  69.5 1.2 %copy.18 = f32[4,1,64,2,256]{4,3,2,1,0:T(2,128)} copy(f32[4,1,64,2,256]{4,2,0,3,1:T(8,128)S(1)} %bitcast.27) | data formatting | bytes 1048576
  70.7 0.6 copy.21
  71.4 0.6 copy.22
  (1 shorter events, 0.0 us)
Async XLA Ops:
  0.6 2.1 %copy-start.5 = (f32[4,1,64,2,256]{4,3,2,1,0:T(2,128)S(1)}, f32[4,1,64,2,256]{4,3,2,1,0:T(2,128)}, u32[]{:S(2)}) copy-start(f32[4,1,64,2,256]{4,3,2,1,0:T(2,128)} %param.12) | copy-start | bytes 1572868
  1.7 1.3 %copy-start = (bf16[4,1,64,1728]{3,2,1,0:T(8,128)(2,1)S(1)}, bf16[4,1,64,1728]{3,2,1,0:T(8,128)(2,1)}, u32[]{:S(2)}) copy-start(bf16[4,1,64,1728]{3,2,1,0:T(8,128)(2,1)} %param.8) | copy-start | bytes 2654212
  2.8 1.0 %copy-start.1 = (bf16[4,1,64,512]{3,2,1,0:T(8,128)(2,1)S(1)}, bf16[4,1,64,512]{3,2,1,0:T(8,128)(2,1)}, u32[]{:S(2)}) copy-start(bf16[4,1,64,512]{3,2,1,0:T(8,128)(2,1)} %param.14) | copy-start | bytes 786436
  2.8 1.1 %copy-start.2 = (s32[4,1,64,256]{3,2,1,0:T(8,128)S(1)}, s32[4,1,64,256]{3,2,1,0:T(8,128)}, u32[]{:S(2)}) copy-start(s32[4,1,64,256]{3,2,1,0:T(8,128)} %param.15) | copy-start | bytes 786436
  2.8 1.1 %copy-start.3 = (s32[4,1,27]{2,1,0:T(1,128)S(1)}, s32[4,1,27]{2,1,0:T(1,128)}, u32[]{:S(2)}) copy-start(s32[4,1,27]{2,1,0:T(1,128)} %param.9) | copy-start | bytes 1300
  2.9 1.0 %copy-start.4 = (f32[4]{0:T(128)S(1)}, f32[4]{0:T(128)}, u32[]{:S(2)}) copy-start(f32[4]{0:T(128)} %coefs.1) | copy-start | bytes 52
